TPU v7x, 32 devices: a whole 2x2x4 slice. The times are simulated.
32 devices in a mesh: ep: 4 (over y, x), fsdp: 8 (over z, core).
Axes of the slice: x: 2, y: 2, z: 4, core: 2. Of those that a mesh axis runs over, the one named last changes fastest.
Arguments:
- tokens: bfloat16 [512, 6144], P('ep', 'fsdp'), may hold values from -6 to 6
- expert_ids: int32 [512, 2], P('ep'), may hold values from 0 to 3, all different within a row; in each aligned block of 128 rows (0 to 127, 128 to 255, ...) at most 128 rows name the same one
- combine_weights: float32 [512, 2], P('ep'), may hold values from 0.25 to 1
- w_gate: bfloat16 [4, 6144, 8192], P('ep', None, 'fsdp'), may hold values from -0.078125 to 0.078125
- w_up: bfloat16 [4, 6144, 8192], P('ep', None, 'fsdp'), may hold values from -0.078125 to 0.078125
- w_down: bfloat16 [4, 8192, 6144], P('ep', 'fsdp'), may hold values from -0.0625 to 0.0625
Outputs:
- mixed_rows: bfloat16 [512, 6144], P('ep', 'fsdp')
Inputs may be any that keep to these rules, and one draw needn't show every extreme that they name: `expert_ids`: among the 128 tokens of one index of ep (aligned blocks of rows), no expert is named by more than 128 rows, a bound that some block reaches; a token names two different experts.
All inputs are finite; a program needn't handle non-finite values.
Results may differ from a plain program's by a relative error of at most 0.0057.
Values may be sent and summed in bfloat16 or wider, within the bound.
A program may use at most 128 MiB of HBM per device.

v0:
```python
import jax
import jax.numpy as jnp
from jax import lax
from jax.sharding import PartitionSpec as P


def shards(tokens, expert_ids, combine_weights, w_gate, w_up, w_down):
    groups = lax.axis_size("ep")
    tok_rows = tokens.shape[0]
    width_local = tokens.shape[1]
    capacity = min(tok_rows, 4 * tok_rows // groups)
    experts_all = groups * w_gate.shape[0]
    chosen = expert_ids.reshape(-1)
    expert_lane = jnp.arange(experts_all, dtype=jnp.int32)
    onehot = (chosen[:, None] == expert_lane[None, :]).astype(jnp.int32)
    before = jnp.cumsum(onehot, axis=0, dtype=jnp.int32) - onehot
    slot_index = jnp.sum(before * onehot, axis=1)
    position = (chosen * capacity + slot_index).reshape(tok_rows, 2)
    places = jnp.arange(experts_all * capacity, dtype=jnp.int32)
    select = position[:, :, None] == places[None, None, :]
    dispatch = jnp.sum(select.astype(jnp.float32), axis=1).astype(jnp.bfloat16)
    packed = lax.dot_general(
        dispatch, tokens, (((0,), (0,)), ((), ())), preferred_element_type=jnp.float32
    )
    packed = packed.astype(jnp.bfloat16).reshape(experts_all, capacity, width_local)
    arrived = lax.all_to_all(packed, "ep", split_axis=0, concat_axis=0, tiled=True)
    expert_rows = arrived.reshape(groups * capacity, width_local)
    gate_local = w_gate[0]
    up_local = w_up[0]
    down_local = w_down[0]
    section = lax.all_gather(expert_rows, "fsdp", axis=1, tiled=True)
    gate_sums = jnp.dot(section, gate_local, preferred_element_type=jnp.float32)
    up_sums = jnp.dot(section, up_local, preferred_element_type=jnp.float32)
    hidden = (jax.nn.silu(gate_sums) * up_sums).astype(jnp.bfloat16)
    summed = lax.psum_scatter(
        lax.dot_general(
            down_local, hidden, (((0,), (1,)), ((), ())), preferred_element_type=jnp.float32
        ),
        "fsdp",
        scatter_dimension=0,
        tiled=True,
    )
    result = summed.T.astype(jnp.bfloat16)
    returned = lax.all_to_all(
        result.reshape(groups, capacity, width_local), "ep", split_axis=0, concat_axis=0, tiled=True
    )
    weighting = jnp.sum(jnp.where(select, combine_weights[:, :, None], 0.0), axis=1)
    mixed_rows = jnp.dot(
        weighting,
        returned.reshape(-1, width_local).astype(jnp.float32),
        precision=lax.Precision.HIGHEST,
    )
    return mixed_rows.astype(jnp.bfloat16)


def solution(mesh):
    in_specs = (
        P("ep", "fsdp"),
        P("ep", None),
        P("ep", None),
        P("ep", None, "fsdp"),
        P("ep", None, "fsdp"),
        P("ep", "fsdp", None),
    )
    out_specs = P("ep", "fsdp")
    return jax.shard_map(shards, mesh=mesh, in_specs=in_specs, out_specs=out_specs, check_vma=False)
```

profile of v0, /device:TPU:0, one launch (start us, length us, event | category | flops | bytes accessed | tf_op | source)
XLA Modules:
  0.0 273.8 jit_solution(12589700919765528524)
XLA Ops:
  6.5 0.0 copy-start
  6.5 0.0 all-gather.2.cloned.1.call-start
  6.5 0.8 copy.25
  7.4 0.1 eq.42
  7.5 0.1 eq.38
  7.7 1.2 reduce-window.6
  8.9 0.1 slice.8
  9.0 0.1 copy.27
  9.1 0.1 copy.28
  9.2 0.1 add_bitcast_fusion
  9.3 0.1 reduce_sum.30
  9.4 0.1 copy.29
  9.5 0.7 multiply_add_fusion
  10.2 0.9 convert_reduce_fusion
  11.1 0.0 copy-done
  11.1 0.4 convolution_convert_fusion
  11.5 16.4 %all_to_all.10 = bf16[4,128,768]{2,1,0:T(8,128)(2,1)} all-to-all(bf16[4,128,768]{2,1,0:T(8,128)(2,1)S(1)} %bitcast.49), channel_id=1, replica_groups=mesh['ep'=4,'fsdp'=8] {'ep'}, dimensions={0} | all-to-all | bytes 1572864 | tf_op jit(solution)/shard_map/all_to_all | solution.py:26
  27.9 0.0 all-gather.2.cloned.1.call-update
  27.9 0.0 reduce-scatter.2.cloned.1.call-start
  28.0 64.5 %all-gather.2.cloned.1.call-done = bf16[512,6144]{1,0:T(8,128)(2,1)} async-done(((bf16[512,768]{1,0:T(8,128)(2,1)}), bf16[512,6144]{1,0:T(8,128)(2,1)}) %all-gather.2.cloned.1.call-update) | async-done | bytes 6291472 | tf_op jit(solution)/shard_map/all_gather | solution.py:31
  92.5 0.0 copy-start.1
  92.5 0.0 slice-start
  92.5 0.0 slice-start.1
  92.5 11.6 %fusion.2 = f32[512,1024]{1,0:T(8,128)S(1)} fusion(bf16[512,6144]{1,0:T(8,128)(2,1)} %all-gather.2.cloned.1.call-done, bf16[1,6144,1024]{2,1,0:T(8,128)(2,1)} %param.10), kind=kOutput, calls=%fused_computation.2 | convolution fusion | flops 6442450944 | bytes 20971520 | tf_op jit(solution)/shard_map/dot_general | solution.py:33
  104.1 0.0 copy-done.1
  104.1 0.0 slice-start.2
  104.1 10.2 %multiply_convert_fusion = bf16[512,1024]{1,0:T(8,128)(2,1)S(1)} fusion(f32[512,1024]{1,0:T(8,128)S(1)} %fusion.2, bf16[512,6144]{1,0:T(8,128)(2,1)S(1)} %copy-done.1, bf16[1,6144,1024]{2,1,0:T(8,128)(2,1)} %param.9), kind=kOutput, calls=%fused_computation.7 | convolution fusion | flops 6445596672 | bytes 22020096 | tf_op jit(solution)/shard_map/dot_general | solution.py:32
  114.4 0.0 slice-done
  114.4 0.0 slice-done.1
  114.4 0.0 slice-done.2
  114.4 9.2 %fusion.6 = f32[6144,512]{0,1:T(8,128)} fusion(bf16[512,1024]{1,0:T(8,128)(2,1)S(1)} %multiply_convert_fusion, bf16[1,1024,6144]{2,1,0:T(8,128)(2,1)S(1)} %bitcast.53), kind=kOutput, calls=%fused_computation.6 | convolution fusion | flops 6442450944 | bytes 26214400 | tf_op jit(solution)/shard_map/dot_general | solution.py:36
  123.6 0.0 reduce-scatter.2.cloned.1.call-update
  123.6 128.1 %reduce-scatter.2.cloned.1.call-done = f32[768,512]{0,1:T(8,128)} async-done(((f32[6144,512]{0,1:T(8,128)}), f32[768,512]{0,1:T(8,128)}) %reduce-scatter.2.cloned.1.call-update) | async-done | bytes 1572880 | tf_op jit(solution)/shard_map/reduce_scatter | solution.py:35
  251.7 1.5 convert_element_type.35
  253.1 12.6 %all_to_all.11 = bf16[4,128,768]{2,1,0:T(8,128)(2,1)S(1)} all-to-all(bf16[4,128,768]{2,1,0:T(8,128)(2,1)S(1)} %bitcast.50), channel_id=1, replica_groups=mesh['ep'=4,'fsdp'=8] {'ep'}, dimensions={0} | all-to-all | bytes 1572864 | tf_op jit(solution)/shard_map/all_to_all | solution.py:44
  265.8 1.2 convolution_convert_fusion.1
  (5 shorter events, 0.1 us)
Async XLA Ops:
  6.5 4.6 %copy-start = (bf16[128,768]{1,0:T(8,128)(2,1)S(1)}, bf16[128,768]{1,0:T(8,128)(2,1)}, u32[]{:S(2)}) copy-start(bf16[128,768]{1,0:T(8,128)(2,1)} %param.6) | copy-start | bytes 589828
  6.5 86.0 %all-gather.2.cloned.1.call-start = ((), (), s32[]{:S(2)}) async-start(), calls=%async_computation.3 | async-start | bytes 7077888 | tf_op jit(solution)/shard_map/all_gather | solution.py:31
  27.9 223.7 %reduce-scatter.2.cloned.1.call-start = ((), (), s32[]{:S(2)}) async-start(), calls=%async_computation.4 | async-start | bytes 14155776 | tf_op jit(solution)/shard_map/reduce_scatter | solution.py:35
  92.5 11.6 %copy-start.1 = (bf16[512,6144]{1,0:T(8,128)(2,1)S(1)}, bf16[512,6144]{1,0:T(8,128)(2,1)}, u32[]{:S(2)}) copy-start(bf16[512,6144]{1,0:T(8,128)(2,1)} %all-gather.2.cloned.1.call-done) | copy-start | bytes 18874372
  92.5 21.8 %slice-start = ((s8[12582912]{0:T(1024)(128)(4,1)}), s8[4194304]{0:T(1024)(128)(4,1)S(1)}, s32[]{:S(2)}) async-start(s8[12582912]{0:T(1024)(128)(4,1)} %bitcast.52), calls=%async_computation.5 | async-start | bytes 8388608
  92.5 21.9 %slice-start.1 = ((s8[12582912]{0:T(1024)(128)(4,1)}), s8[4194304]{0:T(1024)(128)(4,1)S(1)}, s32[]{:S(2)}) async-start(s8[12582912]{0:T(1024)(128)(4,1)} %bitcast.52), calls=%async_computation.6 | async-start | bytes 8388608
  104.1 10.3 %slice-start.2 = ((s8[12582912]{0:T(1024)(128)(4,1)}), s8[4194304]{0:T(1024)(128)(4,1)S(1)}, s32[]{:S(2)}) async-start(s8[12582912]{0:T(1024)(128)(4,1)} %bitcast.52), calls=%async_computation.7 | async-start | bytes 8388608
Sparse Core Ops, SparseCore 0:
  28.0 64.4 all-gather.1
  123.7 127.9 reduce-scatter.1
where the time goes:
time: 274 us
  waiting for transfers between devices  193 us (70%)
  matrix products  32.5 us (12%)
  blocking collectives  29 us (11%)
  between operations  13.5 us (5%)
  other arithmetic  4.43 us (2%)
    reduce_scatter x1, waiting for transfers between devices, shards(): lax.psum_scatter(lax.dot_general(down_local, hidden, (((0,), (1,)), ((),...  128 us
    all_gather x1, waiting for transfers between devices, shards(): section = lax.all_gather(expert_rows, 'fsdp', axis=1, tiled=True)  64.5 us
    all_to_all x1, blocking collectives, shards(): lax.all_to_all(packed, 'ep', split_axis=0, concat_axis=0, tiled=True)  16.4 us
    all_to_all x1, blocking collectives, shards(): lax.all_to_all(result.reshape(groups, capacity, width_local), 'ep', split...  12.6 us
    dot_general x1, matrix products, shards(): up_sums = jnp.dot(section, up_local, preferred_element_type=jnp.float32)  11.6 us
    dot_general x1, matrix products, shards(): gate_sums = jnp.dot(section, gate_local, preferred_element_type=jnp.float32)  10.2 us
    dot_general x1, matrix products, shards(): lax.dot_general(down_local, hidden, (((0,), (1,)), ((), ())), preferred_e...  9.17 us
  transfers between devices with their start and end apart: 2, of which 2 were waited for; matrix products, arithmetic and copies ran while one was open for 0% of the time, Pallas kernels for 0%

commit v1 on v0

--- a/solution.py
+++ b/solution.py
@@ -1,7 +1,298 @@
 import jax
 import jax.numpy as jnp
 from jax import lax
+from jax.experimental import pallas as pl
+from jax.experimental.pallas import tpu as pltpu
 from jax.sharding import PartitionSpec as P
+
+MESH = pl.DeviceIdType.MESH
+BF16 = jnp.bfloat16
+F32 = jnp.float32
+
+
+def kernel(
+    tok, ids, wts, wg, wu, wd, out,
+    rows_all, hid, wg_v, wu_v, wd_v, wt, wcol, acc,
+    sib_r, s1s, s1r, s2s, s2r, s3s, s3r,
+    load_sem, own_sem, ag_send_own, ag_send, ag_sib, ag_recv,
+    wt_send, wt_recv, sib_ss, sib_rs, s1_ss, s1_rs, s2_ss, s2_rs, s3_ss, s3_rs,
+):
+    tok_rows, width = tok.shape
+    half = tok_rows // 2
+    ep = lax.axis_index("ep")
+    fs = lax.axis_index("fsdp")
+    y, x = ep // 2, ep % 2
+    z, c = fs // 2, fs % 2
+    group = [ep, ep + 1 - 2 * x, ep + 2 - 4 * y, 3 - ep]
+
+    def sec(k, plane):
+        core = c if plane == 0 else 1 - c
+        return ((z + k) % 4) * 2 + core
+
+    sib = (ep, z * 2 + 1 - c)
+    x_nbr, y_nbr, diag = (group[1], fs), (group[2], fs), (group[3], fs)
+    z_dev = [None] + [(ep, sec(k, 0)) for k in (1, 2, 3)]
+
+    loads = [
+        pltpu.make_async_copy(wg.at[0], wg_v, load_sem.at[0]),
+        pltpu.make_async_copy(wu.at[0], wu_v, load_sem.at[1]),
+        pltpu.make_async_copy(wd.at[0], wd_v, load_sem.at[2]),
+    ]
+    loads[0].start()
+    loads[1].start()
+
+    def grows(r, h):
+        return pl.ds(pl.multiple_of(group[r] * tok_rows + h * half, half), half)
+
+    def cols(s):
+        return pl.ds(pl.multiple_of(s * width, 128), width)
+
+    def block(r, h, k, plane):
+        return rows_all.at[grows(r, h), cols(sec(k, plane))]
+
+    own = pltpu.make_async_copy(
+        tok,
+        rows_all.at[pl.ds(pl.multiple_of(ep * tok_rows, tok_rows), tok_rows), cols(sec(0, 0))],
+        own_sem,
+    )
+    own.start()
+
+    lane_e = lax.broadcasted_iota(jnp.int32, (8, tok_rows), 0)
+    wt[0] = jnp.where(ids[0:1, :] == lane_e, wts[0:1, :], 0.0) + jnp.where(
+        ids[1:2, :] == lane_e, wts[1:2, :], 0.0
+    )
+
+    barrier = pltpu.get_barrier_semaphore()
+    partners = [sib, x_nbr, y_nbr, diag, z_dev[1], z_dev[2], z_dev[3]]
+    for dev in partners:
+        pl.semaphore_signal(barrier, inc=1, device_id=dev, device_id_type=MESH)
+    pl.semaphore_wait(barrier, len(partners))
+
+    def rcopy(src, dst, ss, rs, dev):
+        return pltpu.make_async_remote_copy(
+            src_ref=src, dst_ref=dst, send_sem=ss, recv_sem=rs, device_id=dev, device_id_type=MESH
+        )
+
+    sent = []
+
+    def send(src, dst, ss, rs, dev):
+        d = rcopy(src, dst, ss, rs, dev)
+        d.start()
+        sent.append(d)
+
+    def rsem(h, r, k, plane):
+        return ag_recv.at[((h * 4 + r) * 4 + k) * 2 + plane]
+
+    def src_of(r, h, k):
+        if r == 0 and k == 0:
+            return tok.at[pl.ds(h * half, half)]
+        return block(r, h, k, 0)
+
+    def to_x(r, h, k):
+        send(src_of(r, h, k), block(r, h, k, 0), ag_send.at[(0 * 2 + h) * 16 + r * 4 + k], rsem(h, r ^ 1, k, 0), x_nbr)
+
+    def to_y(r, h, k):
+        send(src_of(r, h, k), block(r, h, k, 0), ag_send.at[(1 * 2 + h) * 16 + r * 4 + k], rsem(h, r ^ 2, k, 0), y_nbr)
+
+    def to_sib(r, h, k):
+        send(src_of(r, h, k), block(r, h, k, 0), ag_sib.at[h * 16 + r * 4 + k], rsem(h, r, k, 1), sib)
+
+    def arrived(r, h, k, plane):
+        b = block(r, h, k, plane)
+        rcopy(b, b, ag_send.at[0], rsem(h, r, k, plane), sib).wait_recv()
+
+    for h in (0, 1):
+        to_x(0, h, 0)
+        to_y(0, h, 0)
+        for k in (1, 2, 3):
+            send(
+                src_of(0, h, 0), block(0, h, 0, 0), ag_send_own.at[h * 4 + k],
+                rsem(h, 0, 4 - k, 0), z_dev[k],
+            )
+    for i, dev in ((1, x_nbr), (2, y_nbr), (3, diag)):
+        send(wt.at[0], wt.at[i], wt_send.at[i], wt_recv.at[i], dev)
+    for h in (0, 1):
+        to_sib(0, h, 0)
+    loads[2].start()
+
+    def pass_on(k):
+        arrived(1, 0, k, 0)
+        to_y(1, 0, k)
+        arrived(2, 1, k, 0)
+        to_x(2, 1, k)
+        to_sib(1, 0, k)
+        to_sib(2, 1, k)
+
+    for k in (1, 3, 2):
+        for h in (0, 1):
+            arrived(0, h, k, 0)
+            to_x(0, h, k)
+            to_y(0, h, k)
+            to_sib(0, h, k)
+        if k == 1:
+            pass_on(0)
+    for k in (1, 3, 2):
+        pass_on(k)
+    for k in (0, 1, 3, 2):
+        for r, h in ((2, 0), (1, 1), (3, 0), (3, 1)):
+            arrived(r, h, k, 0)
+            to_sib(r, h, k)
+
+    eye = lax.broadcasted_iota(jnp.int32, (tok_rows, tok_rows), 0) == lax.broadcasted_iota(
+        jnp.int32, (tok_rows, tok_rows), 1
+    )
+    for r in range(4):
+        if r > 0:
+            rcopy(wt.at[r], wt.at[r], wt_send.at[0], wt_recv.at[r], sib).wait_recv()
+        row = jnp.sum(jnp.where(lane_e == ep, wt[r], 0.0), axis=0, keepdims=True)
+        col = jnp.sum(jnp.where(eye, row, 0.0), axis=1, keepdims=True)
+        at = pl.ds(pl.multiple_of(group[r] * tok_rows, tok_rows), tok_rows)
+        wcol[at, :] = jnp.broadcast_to(col, (tok_rows, 128))
+
+    for r in range(4):
+        for h in (0, 1):
+            for k in range(4):
+                arrived(r, h, k, 1)
+    own.wait()
+    for d in sent:
+        d.wait_send()
+    sent.clear()
+
+    loads[0].wait()
+    loads[1].wait()
+    tile = 256
+
+    @pl.loop(0, hid.shape[1] // tile)
+    def _(i):
+        at = pl.ds(pl.multiple_of(i * tile, tile), tile)
+        g = jnp.dot(rows_all[...], wg_v[:, at], preferred_element_type=F32)
+        u = jnp.dot(rows_all[...], wu_v[:, at], preferred_element_type=F32)
+        hid[:, at] = (g / (1.0 + jnp.exp(-g)) * u).astype(BF16)
+
+    loads[2].wait()
+
+    def down(s, put):
+        @pl.loop(0, width // tile)
+        def _(i):
+            off = pl.multiple_of(i * tile, tile)
+            at = pl.ds(pl.multiple_of(s * width + i * tile, tile), tile)
+            p = jnp.dot(hid[...], wd_v[:, at], preferred_element_type=F32)
+            put(off, at, p * wcol[:, 0:1])
+
+    steps = (1, 2, 3, 0)
+
+    def stage0(j):
+        k = steps[j]
+
+        def put_sib(off, at, p):
+            rows_all[:, at] = p.astype(BF16)
+
+        def put_own(off, at, p):
+            acc[j, :, pl.ds(off, tile)] = p
+
+        down(sec(k, 1), put_sib)
+        send(rows_all.at[:, cols(sec(k, 1))], sib_r.at[j], sib_ss.at[j], sib_rs.at[j], sib)
+        down(sec(k, 0), put_own)
+
+    def took(dst, rs):
+        rcopy(dst, dst, ag_send.at[0], rs, sib).wait_recv()
+
+    def stage1(j):
+        took(sib_r.at[j], sib_rs.at[j])
+        for h, gone, dev in ((0, (2, 3), y_nbr), (1, (1, 3), x_nbr)):
+            for i, r in enumerate(gone):
+                at = grows(r, h)
+                s1s[j, h, i] = (acc[j, at, :] + sib_r[j, at, :].astype(F32)).astype(BF16)
+            send(s1s.at[j, h], s1r.at[j, h], s1_ss.at[j * 2 + h], s1_rs.at[j * 2 + h], dev)
+        for h, kept in ((0, (0, 1)), (1, (0, 2))):
+            for r in kept:
+                at = grows(r, h)
+                acc[j, at, :] = acc[j, at, :] + sib_r[j, at, :].astype(F32)
+
+    def stage2(j):
+        for h, r, dev in ((0, 1, x_nbr), (1, 2, y_nbr)):
+            took(s1r.at[j, h], s1_rs.at[j * 2 + h])
+            s2s[j, h] = (acc[j, grows(r, h), :] + s1r[j, h, 1].astype(F32)).astype(BF16)
+            send(s2s.at[j, h], s2r.at[j, h], s2_ss.at[j * 2 + h], s2_rs.at[j * 2 + h], dev)
+
+    def stage3(j):
+        k = steps[j]
+        for h in (0, 1):
+            took(s2r.at[j, h], s2_rs.at[j * 2 + h])
+            v = acc[j, grows(0, h), :] + s1r[j, h, 0].astype(F32) + s2r[j, h].astype(F32)
+            if k != 0:
+                s3s[j, h] = v.astype(BF16)
+                send(s3s.at[j, h], s3r.at[j, h], s3_ss.at[j * 2 + h], s3_rs.at[j * 2 + h], z_dev[k])
+            else:
+                for i in range(3):
+                    took(s3r.at[i, h], s3_rs.at[i * 2 + h])
+                    v = v + s3r[i, h].astype(F32)
+                out[pl.ds(h * half, half), :] = v.astype(BF16)
+
+    stage0(0)
+    stage1(0)
+    stage0(1)
+    stage1(1)
+    stage2(0)
+    stage0(2)
+    stage1(2)
+    stage2(1)
+    stage0(3)
+    stage1(3)
+    stage3(0)
+    stage2(2)
+    stage3(1)
+    stage2(3)
+    stage3(2)
+    stage3(3)
+    for d in sent:
+        d.wait_send()
+
+
+def fused(tokens, expert_ids, combine_weights, w_gate, w_up, w_down):
+    tok_rows, width = tokens.shape
+    model = w_gate.shape[1]
+    hidden = w_gate.shape[2]
+    total = 4 * tok_rows
+    half = tok_rows // 2
+    vm = pl.BlockSpec(memory_space=pltpu.VMEM)
+    hbm = pl.BlockSpec(memory_space=pl.ANY)
+    dma = lambda n: pltpu.SemaphoreType.DMA((n,))
+    return pl.pallas_call(
+        kernel,
+        out_shape=jax.ShapeDtypeStruct((tok_rows, width), BF16),
+        in_specs=[vm, vm, vm, hbm, hbm, hbm],
+        out_specs=vm,
+        scratch_shapes=[
+            pltpu.VMEM((total, model), BF16),
+            pltpu.VMEM((total, hidden), BF16),
+            pltpu.VMEM((model, hidden), BF16),
+            pltpu.VMEM((model, hidden), BF16),
+            pltpu.VMEM((hidden, model), BF16),
+            pltpu.VMEM((4, 8, tok_rows), F32),
+            pltpu.VMEM((total, 128), F32),
+            pltpu.VMEM((4, total, width), F32),
+            pltpu.VMEM((4, total, width), BF16),
+            pltpu.VMEM((4, 2, 2, half, width), BF16),
+            pltpu.VMEM((4, 2, 2, half, width), BF16),
+            pltpu.VMEM((4, 2, half, width), BF16),
+            pltpu.VMEM((4, 2, half, width), BF16),
+            pltpu.VMEM((3, 2, half, width), BF16),
+            pltpu.VMEM((3, 2, half, width), BF16),
+            dma(3),
+            pltpu.SemaphoreType.DMA,
+            dma(8), dma(64), dma(32), dma(64),
+            dma(4), dma(4), dma(4), dma(4), dma(8), dma(8), dma(8), dma(8), dma(6), dma(6),
+        ],
+        compiler_params=pltpu.CompilerParams(
+            collective_id=0, has_side_effects=True, vmem_limit_bytes=63 * 1024 * 1024
+        ),
+        cost_estimate=pl.CostEstimate(
+            flops=6 * total * model * hidden,
+            bytes_accessed=6 * model * hidden,
+            transcendentals=total * hidden,
+        ),
+    )(tokens, expert_ids.T, combine_weights.T, w_gate, w_up, w_down)
 
 
 def shards(tokens, expert_ids, combine_weights, w_gate, w_up, w_down):
@@ -63,4 +354,9 @@
         P("ep", "fsdp", None),
     )
     out_specs = P("ep", "fsdp")
-    return jax.shard_map(shards, mesh=mesh, in_specs=in_specs, out_specs=out_specs, check_vma=False)
+
+    def layer(tokens, *rest):
+        small = mesh.shape["ep"] == 4 and mesh.shape["fsdp"] == 8
+        return (fused if small else shards)(tokens, *rest)
+
+    return jax.shard_map(layer, mesh=mesh, in_specs=in_specs, out_specs=out_specs, check_vma=False)

time: 274 us -> 99.1 us (0.36)
  waiting for transfers between devices: 193 us -> 0 us
  Pallas kernels: 0 us -> 97.3 us
  matrix products: 32.5 us -> 0 us
  blocking collectives: 29 us -> 0 us
  between operations: 13.5 us -> 0.01 us
  other arithmetic: 4.43 us -> 0 us
    reduce_scatter x1 -> x0, waiting for transfers between devices: 128 us -> none  [shards(): lax.psum_scatter(lax.dot_general(down_local, hidden, (((0,), (1,)), ((),...]
    pallas_call x0 -> x1, Pallas kernels: none -> 97.3 us  [fused(): pl.pallas_call(kernel, out_shape=jax.ShapeDtypeStruct((tok_rows, width),...]
    all_gather x1 -> x0, waiting for transfers between devices: 64.5 us -> none  [shards(): section = lax.all_gather(expert_rows, 'fsdp', axis=1, tiled=True)]
    dot_general x5 -> x0, matrix products: 32.5 us -> none  [the longest x1 11.6 us: shards(): up_sums = jnp.dot(section, up_local, preferred_element_type=jnp.float32)]
    all_to_all x2 -> x0, blocking collectives: 29 us -> none  [the longest x1 16.4 us: shards(): lax.all_to_all(packed, 'ep', split_axis=0, concat_axis=0, tiled=True)]
  transfers between devices with their start and end apart: 2 -> 0, of which waited for: 2 -> 0; matrix products, arithmetic and copies ran while one was open for 0% -> 0% of each run, Pallas kernels for 0% -> 0%
where the time goes in v1:
time: 99.1 us; the launch traced here: 99 us
  Pallas kernels  97.3 us (98%)
  local copies, waits for them, and re-layouts  1.62 us (2%)
    pallas_call x1, Pallas kernels, fused(): pl.pallas_call(kernel, out_shape=jax.ShapeDtypeStruct((tok_rows, width),...  97.3 us

profile of v1, /device:TPU:0, one launch (start us, length us, event | category | flops | bytes accessed | tf_op | source)
XLA Modules:
  0.0 99.0 jit_solution(2264110122969829741)
XLA Ops:
  0.0 97.3 %shard_map.64 = bf16[128,768]{1,0:T(8,128)(2,1)} custom-call(bf16[128,768]{1,0:T(8,128)(2,1)} %tok.1, s32[2,128]{1,0:T(2,128)} %bitcast.2, f32[2,128]{1,0:T(2,128)} %bitcast.3, bf16[1,6144,1024]{2,1,0:T(8,128)(2,1)} %wg.1, bf16[1,6144,1024]{2,1,0:T(8,128)(2,1)} %wu.1, bf16[1,1024,6144]{2,1,0:T(8,128)(2,1)} %wd.1), custom_call_target="tpu_custom_call" | custom-call | flops 19327352832 | bytes 37748736 | tf_op jit(solution)/shard_map/pallas_call | solution.py:261
  97.3 1.6 %copy.8 = bf16[128,768]{1,0:T(8,128)(2,1)} copy(bf16[128,768]{1,0:T(8,128)(2,1)} %shard_map.64) | data formatting | bytes 393216

commit v2 on v0

--- a/solution.py
+++ b/solution.py
@@ -1,7 +1,355 @@
 import jax
 import jax.numpy as jnp
 from jax import lax
+from jax.experimental import pallas as pl
+from jax.experimental.pallas import tpu as pltpu
 from jax.sharding import PartitionSpec as P
+
+MESH = pl.DeviceIdType.MESH
+BF16 = jnp.bfloat16
+F32 = jnp.float32
+
+
+def kernel(
+    tok, ids, wts, wg, wu, wd, out,
+    rows_all, hid, wg_v, wu_v, wd_v, wt, wcol, acc,
+    sib_r, s1s, s1r, s2s, s2r, s3s, s3r,
+    load_sem, own_sem, ag_send_own, ag_send, ag_sib, ag_recv,
+    wt_send, wt_recv, sib_ss, sib_rs, s1_ss, s1_rs, s2_ss, s2_rs, s3_ss, s3_rs,
+):
+    tok_rows, width = tok.shape
+    part = tok_rows // 2
+    half = tok_rows // 4
+    ep = lax.axis_index("ep")
+    fs = lax.axis_index("fsdp")
+    y, x = ep // 2, ep % 2
+    z, c = fs // 2, fs % 2
+    group = [ep, ep + 1 - 2 * x, ep + 2 - 4 * y, 3 - ep]
+
+    def sec(k, plane):
+        core = c if plane == 0 else 1 - c
+        return ((z + k) % 4) * 2 + core
+
+    sib = (ep, z * 2 + 1 - c)
+    x_nbr, y_nbr, diag = (group[1], fs), (group[2], fs), (group[3], fs)
+    z_dev = [None] + [(ep, sec(k, 0)) for k in (1, 2, 3)]
+
+    loads = [
+        pltpu.make_async_copy(wg.at[0], wg_v, load_sem.at[0]),
+        pltpu.make_async_copy(wu.at[0], wu_v, load_sem.at[1]),
+        pltpu.make_async_copy(wd.at[0], wd_v, load_sem.at[2]),
+    ]
+    loads[0].start()
+    loads[1].start()
+
+    def grows(r, h):
+        return pl.ds(pl.multiple_of(group[r] * part + h * half, half), half)
+
+    def cols(s):
+        return pl.ds(pl.multiple_of(s * width, 128), width)
+
+    def block(b, r, h, k, plane):
+        return rows_all.at[b, grows(r, h), cols(sec(k, plane))]
+
+    own = [
+        pltpu.make_async_copy(
+            tok.at[pl.ds(b * part, part)],
+            rows_all.at[b, pl.ds(pl.multiple_of(ep * part, part), part), cols(sec(0, 0))],
+            own_sem.at[b],
+        )
+        for b in (0, 1)
+    ]
+    own[0].start()
+    own[1].start()
+
+    lane_e = lax.broadcasted_iota(jnp.int32, (8, tok_rows), 0)
+    wt[0] = jnp.where(ids[0:1, :] == lane_e, wts[0:1, :], 0.0) + jnp.where(
+        ids[1:2, :] == lane_e, wts[1:2, :], 0.0
+    )
+
+    barrier = pltpu.get_barrier_semaphore()
+    partners = [sib, x_nbr, y_nbr, diag, z_dev[1], z_dev[2], z_dev[3]]
+    for dev in partners:
+        pl.semaphore_signal(barrier, inc=1, device_id=dev, device_id_type=MESH)
+    pl.semaphore_wait(barrier, len(partners))
+
+    def rcopy(src, dst, ss, rs, dev):
+        return pltpu.make_async_remote_copy(
+            src_ref=src, dst_ref=dst, send_sem=ss, recv_sem=rs, device_id=dev, device_id_type=MESH
+        )
+
+    sent = {0: [], 1: [], 2: []}
+
+    def send(lot, src, dst, ss, rs, dev):
+        d = rcopy(src, dst, ss, rs, dev)
+        d.start()
+        sent[lot].append(d)
+
+    def rsem(b, h, r, k, plane):
+        return ag_recv.at[(((b * 2 + h) * 4 + r) * 4 + k) * 2 + plane]
+
+    def src_of(b, r, h, k):
+        if r == 0 and k == 0:
+            return tok.at[pl.ds(b * part + h * half, half)]
+        return block(b, r, h, k, 0)
+
+    def to_x(b, r, h, k):
+        send(b, src_of(b, r, h, k), block(b, r, h, k, 0),
+             ag_send.at[(b * 2 + h) * 16 + r * 4 + k], rsem(b, h, r ^ 1, k, 0), x_nbr)
+
+    def to_y(b, r, h, k):
+        send(b, src_of(b, r, h, k), block(b, r, h, k, 0),
+             ag_send.at[64 + (b * 2 + h) * 16 + r * 4 + k], rsem(b, h, r ^ 2, k, 0), y_nbr)
+
+    def to_sib(b, r, h, k):
+        send(b, src_of(b, r, h, k), block(b, r, h, k, 0),
+             ag_sib.at[(b * 2 + h) * 16 + r * 4 + k], rsem(b, h, r, k, 1), sib)
+
+    def arrived(b, r, h, k, plane):
+        at = block(b, r, h, k, plane)
+        rcopy(at, at, ag_send.at[0], rsem(b, h, r, k, plane), sib).wait_recv()
+
+    def own_z(b):
+        for h in (0, 1):
+            for k in (1, 2, 3):
+                send(b, src_of(b, 0, h, 0), block(b, 0, h, 0, 0),
+                     ag_send_own.at[(b * 2 + h) * 4 + k], rsem(b, h, 0, 4 - k, 0), z_dev[k])
+
+    def own_xy(b):
+        for h in (0, 1):
+            to_x(b, 0, h, 0)
+            to_y(b, 0, h, 0)
+
+    def own_sib(b):
+        for h in (0, 1):
+            to_sib(b, 0, h, 0)
+
+    def from_z(b, k):
+        for h in (0, 1):
+            arrived(b, 0, h, k, 0)
+            to_x(b, 0, h, k)
+            to_y(b, 0, h, k)
+            to_sib(b, 0, h, k)
+
+    def pass_on(b, k):
+        arrived(b, 1, 0, k, 0)
+        to_y(b, 1, 0, k)
+        arrived(b, 2, 1, k, 0)
+        to_x(b, 2, 1, k)
+        to_sib(b, 1, 0, k)
+        to_sib(b, 2, 1, k)
+
+    def last(b, k):
+        for r, h in ((2, 0), (1, 1), (3, 0), (3, 1)):
+            arrived(b, r, h, k, 0)
+            to_sib(b, r, h, k)
+
+    def gathered(b):
+        for r in range(4):
+            for h in (0, 1):
+                for k in range(4):
+                    arrived(b, r, h, k, 1)
+        own[b].wait()
+
+    def all_sent(lot):
+        for d in sent[lot]:
+            d.wait_send()
+        sent[lot].clear()
+
+    own_z(0)
+    own_xy(0)
+    for i, dev in ((1, x_nbr), (2, y_nbr), (3, diag)):
+        send(2, wt.at[0], wt.at[i], wt_send.at[i], wt_recv.at[i], dev)
+    own_sib(0)
+    own_xy(1)
+    own_sib(1)
+    loads[2].start()
+    from_z(0, 1)
+    pass_on(0, 0)
+    from_z(0, 3)
+    from_z(0, 2)
+    own_z(1)
+    for k in (1, 3, 2):
+        pass_on(0, k)
+    for k in (0, 1, 3, 2):
+        last(0, k)
+
+    eye = lax.broadcasted_iota(jnp.int32, (tok_rows, tok_rows), 0) == lax.broadcasted_iota(
+        jnp.int32, (tok_rows, tok_rows), 1
+    )
+    for r in range(4):
+        if r > 0:
+            rcopy(wt.at[r], wt.at[r], wt_send.at[0], wt_recv.at[r], sib).wait_recv()
+        row = jnp.sum(jnp.where(lane_e == ep, wt[r], 0.0), axis=0, keepdims=True)
+        col = jnp.sum(jnp.where(eye, row, 0.0), axis=1, keepdims=True)
+        at = pl.ds(pl.multiple_of(group[r] * part, part), part)
+        for b in (0, 1):
+            wcol[b, at, :] = jnp.broadcast_to(col[b * part:(b + 1) * part], (part, 128))
+
+    tile = hid.shape[2] // 4
+
+    def up(b, i):
+        at = pl.ds(i * tile, tile)
+        g = jnp.dot(rows_all[b], wg_v[:, at], preferred_element_type=F32)
+        u = jnp.dot(rows_all[b], wu_v[:, at], preferred_element_type=F32)
+        hid[b, :, at] = (g / (1.0 + jnp.exp(-g)) * u).astype(BF16)
+
+    steps = (1, 2, 3, 0)
+
+    def down(b, s):
+        p = jnp.dot(hid[b], wd_v[:, cols(s)], preferred_element_type=F32)
+        return p * wcol[b, :, 0:1]
+
+    def stage0(b, j):
+        k = steps[j]
+        s = cols(sec(k, 1))
+        rows_all[b, :, s] = down(b, sec(k, 1)).astype(BF16)
+        send(2, rows_all.at[b, :, s], sib_r.at[b, j], sib_ss.at[b * 4 + j], sib_rs.at[b * 4 + j], sib)
+        acc[b, j] = down(b, sec(k, 0))
+
+    def took(dst, rs):
+        rcopy(dst, dst, ag_send.at[0], rs, sib).wait_recv()
+
+    def stage1(b, j):
+        took(sib_r.at[b, j], sib_rs.at[b * 4 + j])
+        for h, gone, dev in ((0, (2, 3), y_nbr), (1, (1, 3), x_nbr)):
+            n = (b * 4 + j) * 2 + h
+            for i, r in enumerate(gone):
+                at = grows(r, h)
+                s1s[b, j, h, i] = (acc[b, j, at, :] + sib_r[b, j, at, :].astype(F32)).astype(BF16)
+            send(2, s1s.at[b, j, h], s1r.at[b, j, h], s1_ss.at[n], s1_rs.at[n], dev)
+        for h, kept in ((0, (0, 1)), (1, (0, 2))):
+            for r in kept:
+                at = grows(r, h)
+                acc[b, j, at, :] = acc[b, j, at, :] + sib_r[b, j, at, :].astype(F32)
+
+    def stage2(b, j):
+        for h, r, dev in ((0, 1, x_nbr), (1, 2, y_nbr)):
+            n = (b * 4 + j) * 2 + h
+            took(s1r.at[b, j, h], s1_rs.at[n])
+            s2s[b, j, h] = (acc[b, j, grows(r, h), :] + s1r[b, j, h, 1].astype(F32)).astype(BF16)
+            send(2, s2s.at[b, j, h], s2r.at[b, j, h], s2_ss.at[n], s2_rs.at[n], dev)
+
+    def stage3(b, j):
+        k = steps[j]
+        for h in (0, 1):
+            n = (b * 4 + j) * 2 + h
+            took(s2r.at[b, j, h], s2_rs.at[n])
+            v = acc[b, j, grows(0, h), :] + s1r[b, j, h, 0].astype(F32) + s2r[b, j, h].astype(F32)
+            if k != 0:
+                n = (b * 3 + j) * 2 + h
+                s3s[b, j, h] = v.astype(BF16)
+                send(2, s3s.at[b, j, h], s3r.at[b, j, h], s3_ss.at[n], s3_rs.at[n], z_dev[k])
+            else:
+                for i in range(3):
+                    took(s3r.at[b, i, h], s3_rs.at[(b * 3 + i) * 2 + h])
+                    v = v + s3r[b, i, h].astype(F32)
+                out[pl.ds(b * part + h * half, half), :] = v.astype(BF16)
+
+    for k in (1, 3, 2):
+        from_z(1, k)
+    gathered(0)
+    loads[0].wait()
+    loads[1].wait()
+    up(0, 0)
+    pass_on(1, 0)
+    pass_on(1, 1)
+    up(0, 1)
+    pass_on(1, 3)
+    pass_on(1, 2)
+    up(0, 2)
+    last(1, 0)
+    up(0, 3)
+    last(1, 1)
+    all_sent(0)
+    loads[2].wait()
+    stage0(0, 0)
+    last(1, 3)
+    stage0(0, 1)
+    stage1(0, 0)
+    last(1, 2)
+    stage0(0, 2)
+    stage1(0, 1)
+    stage0(0, 3)
+    stage1(0, 2)
+    stage1(0, 3)
+    gathered(1)
+    up(1, 0)
+    stage2(0, 0)
+    stage2(0, 1)
+    up(1, 1)
+    stage2(0, 2)
+    stage3(0, 0)
+    up(1, 2)
+    stage2(0, 3)
+    stage3(0, 1)
+    up(1, 3)
+    stage3(0, 2)
+    all_sent(1)
+    stage0(1, 0)
+    stage0(1, 1)
+    stage1(1, 0)
+    stage0(1, 2)
+    stage1(1, 1)
+    stage0(1, 3)
+    stage1(1, 2)
+    stage2(1, 0)
+    stage1(1, 3)
+    stage3(0, 3)
+    stage2(1, 1)
+    stage3(1, 0)
+    stage2(1, 2)
+    stage3(1, 1)
+    stage2(1, 3)
+    stage3(1, 2)
+    stage3(1, 3)
+    all_sent(2)
+
+
+def fused(tokens, expert_ids, combine_weights, w_gate, w_up, w_down):
+    tok_rows, width = tokens.shape
+    model = w_gate.shape[1]
+    hidden = w_gate.shape[2]
+    total = 2 * tok_rows
+    half = tok_rows // 4
+    vm = pl.BlockSpec(memory_space=pltpu.VMEM)
+    hbm = pl.BlockSpec(memory_space=pl.ANY)
+    dma = lambda n: pltpu.SemaphoreType.DMA((n,))
+    return pl.pallas_call(
+        kernel,
+        out_shape=jax.ShapeDtypeStruct((tok_rows, width), BF16),
+        in_specs=[vm, vm, vm, hbm, hbm, hbm],
+        out_specs=vm,
+        scratch_shapes=[
+            pltpu.VMEM((2, total, model), BF16),
+            pltpu.VMEM((2, total, hidden), BF16),
+            pltpu.VMEM((model, hidden), BF16),
+            pltpu.VMEM((model, hidden), BF16),
+            pltpu.VMEM((hidden, model), BF16),
+            pltpu.VMEM((4, 8, tok_rows), F32),
+            pltpu.VMEM((2, total, 128), F32),
+            pltpu.VMEM((2, 4, total, width), F32),
+            pltpu.VMEM((2, 4, total, width), BF16),
+            pltpu.VMEM((2, 4, 2, 2, half, width), BF16),
+            pltpu.VMEM((2, 4, 2, 2, half, width), BF16),
+            pltpu.VMEM((2, 4, 2, half, width), BF16),
+            pltpu.VMEM((2, 4, 2, half, width), BF16),
+            pltpu.VMEM((2, 3, 2, half, width), BF16),
+            pltpu.VMEM((2, 3, 2, half, width), BF16),
+            dma(3),
+            dma(2),
+            dma(16), dma(128), dma(64), dma(128),
+            dma(4), dma(4), dma(8), dma(8), dma(16), dma(16), dma(16), dma(16), dma(12), dma(12),
+        ],
+        compiler_params=pltpu.CompilerParams(
+            collective_id=0, has_side_effects=True, vmem_limit_bytes=63 * 1024 * 1024
+        ),
+        cost_estimate=pl.CostEstimate(
+            flops=12 * total * model * hidden,
+            bytes_accessed=6 * model * hidden,
+            transcendentals=2 * total * hidden,
+        ),
+    )(tokens, expert_ids.T, combine_weights.T, w_gate, w_up, w_down)
 
 
 def shards(tokens, expert_ids, combine_weights, w_gate, w_up, w_down):
@@ -63,4 +411,9 @@
         P("ep", "fsdp", None),
     )
     out_specs = P("ep", "fsdp")
-    return jax.shard_map(shards, mesh=mesh, in_specs=in_specs, out_specs=out_specs, check_vma=False)
+
+    def layer(tokens, *rest):
+        small = mesh.shape["ep"] == 4 and mesh.shape["fsdp"] == 8
+        return (fused if small else shards)(tokens, *rest)
+
+    return jax.shard_map(layer, mesh=mesh, in_specs=in_specs, out_specs=out_specs, check_vma=False)

time: 274 us -> 85.3 us (0.31)
  waiting for transfers between devices: 193 us -> 0 us
  Pallas kernels: 0 us -> 83.5 us
  matrix products: 32.5 us -> 0 us
  blocking collectives: 29 us -> 0 us
  between operations: 13.5 us -> 0.01 us
  other arithmetic: 4.43 us -> 0 us
    reduce_scatter x1 -> x0, waiting for transfers between devices: 128 us -> none  [shards(): lax.psum_scatter(lax.dot_general(down_local, hidden, (((0,), (1,)), ((),...]
    pallas_call x0 -> x1, Pallas kernels: none -> 83.5 us  [fused(): pl.pallas_call(kernel, out_shape=jax.ShapeDtypeStruct((tok_rows, width),...]
    all_gather x1 -> x0, waiting for transfers between devices: 64.5 us -> none  [shards(): section = lax.all_gather(expert_rows, 'fsdp', axis=1, tiled=True)]
    dot_general x5 -> x0, matrix products: 32.5 us -> none  [the longest x1 11.6 us: shards(): up_sums = jnp.dot(section, up_local, preferred_element_type=jnp.float32)]
    all_to_all x2 -> x0, blocking collectives: 29 us -> none  [the longest x1 16.4 us: shards(): lax.all_to_all(packed, 'ep', split_axis=0, concat_axis=0, tiled=True)]
  transfers between devices with their start and end apart: 2 -> 0, of which waited for: 2 -> 0; matrix products, arithmetic and copies ran while one was open for 0% -> 0% of each run, Pallas kernels for 0% -> 0%
where the time goes in v2:
time: 85.3 us; the launch traced here: 85.2 us
  Pallas kernels  83.5 us (98%)
  local copies, waits for them, and re-layouts  1.62 us (2%)
    pallas_call x1, Pallas kernels, fused(): pl.pallas_call(kernel, out_shape=jax.ShapeDtypeStruct((tok_rows, width),...  83.5 us

profile of v2, /device:TPU:0, one launch (start us, length us, event | category | flops | bytes accessed | tf_op | source)
XLA Modules:
  0.0 85.2 jit_solution(9919486379039935036)
XLA Ops:
  0.0 83.5 %shard_map.64 = bf16[128,768]{1,0:T(8,128)(2,1)} custom-call(bf16[128,768]{1,0:T(8,128)(2,1)} %tok.1, s32[2,128]{1,0:T(2,128)} %bitcast.2, f32[2,128]{1,0:T(2,128)} %bitcast.3, bf16[1,6144,1024]{2,1,0:T(8,128)(2,1)} %wg.1, bf16[1,6144,1024]{2,1,0:T(8,128)(2,1)} %wu.1, bf16[1,1024,6144]{2,1,0:T(8,128)(2,1)} %wd.1), custom_call_target="tpu_custom_call" | custom-call | flops 19327352832 | bytes 37748736 | tf_op jit(solution)/shard_map/pallas_call | solution.py:318
  83.5 1.6 %copy.8 = bf16[128,768]{1,0:T(8,128)(2,1)} copy(bf16[128,768]{1,0:T(8,128)(2,1)} %shard_map.64) | data formatting | bytes 393216

commit v3 on v2

v3 whole, which is shorter than its diff:
```python
import jax
import jax.numpy as jnp
from jax import lax
from jax.experimental import pallas as pl
from jax.experimental.pallas import tpu as pltpu
from jax.sharding import PartitionSpec as P

MESH = pl.DeviceIdType.MESH
BF16 = jnp.bfloat16
F32 = jnp.float32


def kernel(
    tok, ids, wts, wg, wu, wd, out,
    rows_all, hid, wg_v, wu_v, wd_v, wt, wcol, acc,
    sib_r, s1s, s1r, s2s, s2r, s3s, s3r,
    load_sem, own_sem, z_ss, z_rs, h1_ss, h1_rs, h2_ss, h2_rs, c0_ss, c0_rs, c1_ss, c1_rs,
    wt_send, wt_recv, sib_ss, sib_rs, s1_ss, s1_rs, s2_ss, s2_rs, s3_ss, s3_rs,
):
    tok_rows, width = tok.shape
    part = tok_rows // 2
    half = tok_rows // 4
    ep = lax.axis_index("ep")
    fs = lax.axis_index("fsdp")
    y, x = ep // 2, ep % 2
    z, c = fs // 2, fs % 2
    group = [ep, ep + 1 - 2 * x, ep + 2 - 4 * y, 3 - ep]

    def sec(k, plane):
        core = c if plane == 0 else 1 - c
        return ((z + k) % 4) * 2 + core

    sib = (ep, z * 2 + 1 - c)
    x_nbr, y_nbr, diag = (group[1], fs), (group[2], fs), (group[3], fs)
    z_dev = [None] + [(ep, sec(k, 0)) for k in (1, 2, 3)]

    loads = [
        pltpu.make_async_copy(wg.at[0], wg_v, load_sem.at[0]),
        pltpu.make_async_copy(wu.at[0], wu_v, load_sem.at[1]),
        pltpu.make_async_copy(wd.at[0], wd_v, load_sem.at[2]),
    ]

    def place(r, h):
        gy = y if r < 2 else 1 - y
        gx = x if r % 2 == 0 else 1 - x
        return gy * 2 + gx if h == 0 else gx * 2 + gy

    def grows(r, h):
        return pl.ds(pl.multiple_of(h * part * 2 + place(r, h) * half, half), half)

    def prows(h, other):
        first = y if h == 0 else x
        if other:
            first = 1 - first
        return pl.ds(pl.multiple_of(h * part * 2 + first * part, part), part)

    def cols(s):
        return pl.ds(pl.multiple_of(s * width, 128), width)

    def own_block(b, h, k):
        return rows_all.at[b, grows(0, h), cols(sec(k, 0))]

    def pair(b, h, k, other, plane=0):
        return rows_all.at[b, prows(h, other), cols(sec(k, plane))]

    def tok_part(b, h):
        return tok.at[pl.ds(b * part + h * half, half)]

    both = [(b, h) for b in (0, 1) for h in (0, 1)]
    own = [
        pltpu.make_async_copy(tok_part(b, h), own_block(b, h, 0), own_sem.at[b * 2 + h])
        for b, h in both
    ]
    for d in own:
        d.start()

    lane_e = lax.broadcasted_iota(jnp.int32, (8, tok_rows), 0)
    wt[0] = jnp.where(ids[0:1, :] == lane_e, wts[0:1, :], 0.0) + jnp.where(
        ids[1:2, :] == lane_e, wts[1:2, :], 0.0
    )

    barrier = pltpu.get_barrier_semaphore()
    partners = [sib, x_nbr, y_nbr, diag, z_dev[1], z_dev[2], z_dev[3]]
    for dev in partners:
        pl.semaphore_signal(barrier, inc=1, device_id=dev, device_id_type=MESH)
    loads[0].start()
    loads[1].start()
    for d in own:
        d.wait()
    pl.semaphore_wait(barrier, len(partners))

    def rcopy(src, dst, ss, rs, dev):
        return pltpu.make_async_remote_copy(
            src_ref=src, dst_ref=dst, send_sem=ss, recv_sem=rs, device_id=dev, device_id_type=MESH
        )

    def send(src, dst, ss, rs, dev):
        rcopy(src, dst, ss, rs, dev).start()

    def took(dst, rs):
        rcopy(dst, dst, z_ss.at[0], rs, sib).wait_recv()

    def left(src, ss):
        rcopy(src, src, ss, z_rs.at[0], sib).wait_send()

    def num(b, h, k):
        return (b * 2 + h) * 4 + k

    def own_z(b):
        for h in (0, 1):
            for k in (1, 2, 3):
                send(tok_part(b, h), own_block(b, h, 0), z_ss.at[num(b, h, k)],
                     z_rs.at[num(b, h, 4 - k)], z_dev[k])

    def first(b, k):
        for h, dev in ((0, x_nbr), (1, y_nbr)):
            n = num(b, h, k)
            at = own_block(b, h, k)
            if k != 0:
                took(at, z_rs.at[n])
            send(at, at, h1_ss.at[n], h1_rs.at[n], dev)

    def second(b, k):
        for h, r, dev in ((0, 1, y_nbr), (1, 2, x_nbr)):
            n = num(b, h, k)
            took(rows_all.at[b, grows(r, h), cols(sec(k, 0))], h1_rs.at[n])
            at = pair(b, h, k, False)
            send(at, at, h2_ss.at[n], h2_rs.at[n], dev)
            send(at, at, c0_ss.at[n], c0_rs.at[n], sib)

    def last(b, k):
        for h in (0, 1):
            n = num(b, h, k)
            at = pair(b, h, k, True)
            took(at, h2_rs.at[n])
            send(at, at, c1_ss.at[n], c1_rs.at[n], sib)

    def gathered(b):
        @pl.loop(0, 4)
        def _(k):
            for h in (0, 1):
                took(pair(b, h, k, False, 1), c0_rs.at[num(b, h, k)])
                took(pair(b, h, k, True, 1), c1_rs.at[num(b, h, k)])

    def all_sent(b):
        @pl.loop(0, 4)
        def _(k):
            for h in (0, 1):
                n = num(b, h, k)
                left(own_block(b, h, k), h1_ss.at[n])
                left(pair(b, h, k, False), h2_ss.at[n])
                left(pair(b, h, k, False), c0_ss.at[n])
                left(pair(b, h, k, True), c1_ss.at[n])

        for h in (0, 1):
            for k in (1, 2, 3):
                left(tok_part(b, h), z_ss.at[num(b, h, k)])

    own_z(0)
    first(0, 0)
    for i, dev in ((1, x_nbr), (2, y_nbr), (3, diag)):
        send(wt.at[0], wt.at[i], wt_send.at[i], wt_recv.at[i], dev)
    loads[2].start()
    second(0, 0)
    first(0, 1)
    first(0, 3)
    first(0, 2)
    own_z(1)
    first(1, 0)
    second(0, 1)
    second(0, 3)
    second(0, 2)

    eye = lax.broadcasted_iota(jnp.int32, (tok_rows, tok_rows), 0) == lax.broadcasted_iota(
        jnp.int32, (tok_rows, tok_rows), 1
    )
    for r in range(4):
        if r > 0:
            took(wt.at[r], wt_recv.at[r])
        row = jnp.sum(jnp.where(lane_e == ep, wt[r], 0.0), axis=0, keepdims=True)
        col = jnp.sum(jnp.where(eye, row, 0.0), axis=1, keepdims=True)
        for b, h in both:
            lo = b * part + h * half
            wcol[b, grows(r, h), :] = jnp.broadcast_to(col[lo:lo + half], (half, 128))

    for k in (0, 1, 3, 2):
        last(0, k)
    for k in (1, 3, 2):
        first(1, k)

    tile = hid.shape[2] // 4

    def up(b, i):
        at = pl.ds(pl.multiple_of(i * tile, tile), tile)
        g = jnp.dot(rows_all[b], wg_v[:, at], preferred_element_type=F32)
        u = jnp.dot(rows_all[b], wu_v[:, at], preferred_element_type=F32)
        hid[b, :, at] = (g / (1.0 + jnp.exp(-g)) * u).astype(BF16)

    def down(b, s):
        p = jnp.dot(hid[b], wd_v[:, cols(s)], preferred_element_type=F32)
        return p * wcol[b, :, 0:1]

    def stage0(b, j):
        k = (j + 1) % 4
        s = cols(sec(k, 1))
        n = b * 4 + j
        rows_all[b, :, s] = down(b, sec(k, 1)).astype(BF16)
        send(rows_all.at[b, :, s], sib_r.at[b, j], sib_ss.at[n], sib_rs.at[n], sib)
        acc[b, j] = down(b, sec(k, 0))

    def stage1(b, j):
        took(sib_r.at[b, j], sib_rs.at[b * 4 + j])
        for h, gone, dev in ((0, (2, 3), y_nbr), (1, (1, 3), x_nbr)):
            n = (b * 4 + j) * 2 + h
            for i, r in enumerate(gone):
                at = grows(r, h)
                s1s[b, j, h, i] = (acc[b, j, at, :] + sib_r[b, j, at, :].astype(F32)).astype(BF16)
            send(s1s.at[b, j, h], s1r.at[b, j, h], s1_ss.at[n], s1_rs.at[n], dev)
        for h, kept in ((0, (0, 1)), (1, (0, 2))):
            for r in kept:
                at = grows(r, h)
                acc[b, j, at, :] = acc[b, j, at, :] + sib_r[b, j, at, :].astype(F32)

    def stage2(b, j):
        for h, r, dev in ((0, 1, x_nbr), (1, 2, y_nbr)):
            n = (b * 4 + j) * 2 + h
            took(s1r.at[b, j, h], s1_rs.at[n])
            s2s[b, j, h] = (acc[b, j, grows(r, h), :] + s1r[b, j, h, 1].astype(F32)).astype(BF16)
            send(s2s.at[b, j, h], s2r.at[b, j, h], s2_ss.at[n], s2_rs.at[n], dev)

    def summed(b, j, h):
        took(s2r.at[b, j, h], s2_rs.at[(b * 4 + j) * 2 + h])
        return acc[b, j, grows(0, h), :] + s1r[b, j, h, 0].astype(F32) + s2r[b, j, h].astype(F32)

    def stage3(b, j):
        for h in (0, 1):
            n = (b * 3 + j) * 2 + h
            s3s[b, j, h] = summed(b, j, h).astype(BF16)
            send(s3s.at[b, j, h], s3r.at[b, j, h], s3_ss.at[n], s3_rs.at[n], (ep, sec(j + 1, 0)))

    def finish(b):
        for h in (0, 1):
            v = summed(b, 3, h)
            for i in range(3):
                took(s3r.at[b, i, h], s3_rs.at[(b * 3 + i) * 2 + h])
                v = v + s3r[b, i, h].astype(F32)
            out[pl.ds(b * part + h * half, half), :] = v.astype(BF16)

    gathered(0)
    loads[0].wait()
    loads[1].wait()

    @pl.loop(0, 4)
    def _(i):
        up(0, i)
        second(1, i)

    all_sent(0)
    loads[2].wait()

    @pl.loop(0, 4)
    def _(j):
        stage0(0, j)
        last(1, j)

        @pl.when(j > 0)
        def _():
            stage1(0, j - 1)

    stage1(0, 3)
    gathered(1)

    @pl.loop(0, 4)
    def _(i):
        up(1, i)
        stage2(0, i)

        @pl.when(i > 0)
        def _():
            stage3(0, i - 1)

    all_sent(1)

    @pl.loop(0, 4)
    def _(j):
        stage0(1, j)

        @pl.when(j > 0)
        def _():
            stage1(1, j - 1)

        @pl.when(j > 1)
        def _():
            stage2(1, j - 2)

    stage1(1, 3)
    stage2(1, 2)
    stage3(1, 0)
    finish(0)
    stage3(1, 1)
    stage2(1, 3)
    stage3(1, 2)
    finish(1)

    for i in (1, 2, 3):
        left(wt.at[0], wt_send.at[i])
    for b in (0, 1):
        @pl.loop(0, 4)
        def _(j):
            left(sib_r.at[b, j], sib_ss.at[b * 4 + j])
            for h in (0, 1):
                left(s1s.at[b, j, h], s1_ss.at[(b * 4 + j) * 2 + h])
                left(s2s.at[b, j, h], s2_ss.at[(b * 4 + j) * 2 + h])

        @pl.loop(0, 3)
        def _(j):
            for h in (0, 1):
                left(s3s.at[b, j, h], s3_ss.at[(b * 3 + j) * 2 + h])


def fused(tokens, expert_ids, combine_weights, w_gate, w_up, w_down):
    tok_rows, width = tokens.shape
    model = w_gate.shape[1]
    hidden = w_gate.shape[2]
    total = 2 * tok_rows
    half = tok_rows // 4
    vm = pl.BlockSpec(memory_space=pltpu.VMEM)
    hbm = pl.BlockSpec(memory_space=pl.ANY)
    dma = lambda n: pltpu.SemaphoreType.DMA((n,))
    return pl.pallas_call(
        kernel,
        out_shape=jax.ShapeDtypeStruct((tok_rows, width), BF16),
        in_specs=[vm, vm, vm, hbm, hbm, hbm],
        out_specs=vm,
        scratch_shapes=[
            pltpu.VMEM((2, total, model), BF16),
            pltpu.VMEM((2, total, hidden), BF16),
            pltpu.VMEM((model, hidden), BF16),
            pltpu.VMEM((model, hidden), BF16),
            pltpu.VMEM((hidden, model), BF16),
            pltpu.VMEM((4, 8, tok_rows), F32),
            pltpu.VMEM((2, total, 128), F32),
            pltpu.VMEM((2, 4, total, width), F32),
            pltpu.VMEM((2, 4, total, width), BF16),
            pltpu.VMEM((2, 4, 2, 2, half, width), BF16),
            pltpu.VMEM((2, 4, 2, 2, half, width), BF16),
            pltpu.VMEM((2, 4, 2, half, width), BF16),
            pltpu.VMEM((2, 4, 2, half, width), BF16),
            pltpu.VMEM((2, 3, 2, half, width), BF16),
            pltpu.VMEM((2, 3, 2, half, width), BF16),
            dma(3),
            dma(4),
            dma(16), dma(16), dma(16), dma(16), dma(16), dma(16), dma(16), dma(16), dma(16), dma(16),
            dma(4), dma(4), dma(8), dma(8), dma(16), dma(16), dma(16), dma(16), dma(12), dma(12),
        ],
        compiler_params=pltpu.CompilerParams(
            collective_id=0, has_side_effects=True, vmem_limit_bytes=63 * 1024 * 1024
        ),
        cost_estimate=pl.CostEstimate(
            flops=12 * total * model * hidden,
            bytes_accessed=6 * model * hidden,
            transcendentals=2 * total * hidden,
        ),
    )(tokens, expert_ids.T, combine_weights.T, w_gate, w_up, w_down)


def shards(tokens, expert_ids, combine_weights, w_gate, w_up, w_down):
    groups = lax.axis_size("ep")
    tok_rows = tokens.shape[0]
    width_local = tokens.shape[1]
    capacity = min(tok_rows, 4 * tok_rows // groups)
    experts_all = groups * w_gate.shape[0]
    chosen = expert_ids.reshape(-1)
    expert_lane = jnp.arange(experts_all, dtype=jnp.int32)
    onehot = (chosen[:, None] == expert_lane[None, :]).astype(jnp.int32)
    before = jnp.cumsum(onehot, axis=0, dtype=jnp.int32) - onehot
    slot_index = jnp.sum(before * onehot, axis=1)
    position = (chosen * capacity + slot_index).reshape(tok_rows, 2)
    places = jnp.arange(experts_all * capacity, dtype=jnp.int32)
    select = position[:, :, None] == places[None, None, :]
    dispatch = jnp.sum(select.astype(jnp.float32), axis=1).astype(jnp.bfloat16)
    packed = lax.dot_general(
        dispatch, tokens, (((0,), (0,)), ((), ())), preferred_element_type=jnp.float32
    )
    packed = packed.astype(jnp.bfloat16).reshape(experts_all, capacity, width_local)
    arrived = lax.all_to_all(packed, "ep", split_axis=0, concat_axis=0, tiled=True)
    expert_rows = arrived.reshape(groups * capacity, width_local)
    gate_local = w_gate[0]
    up_local = w_up[0]
    down_local = w_down[0]
    section = lax.all_gather(expert_rows, "fsdp", axis=1, tiled=True)
    gate_sums = jnp.dot(section, gate_local, preferred_element_type=jnp.float32)
    up_sums = jnp.dot(section, up_local, preferred_element_type=jnp.float32)
    hidden = (jax.nn.silu(gate_sums) * up_sums).astype(jnp.bfloat16)
    summed = lax.psum_scatter(
        lax.dot_general(
            down_local, hidden, (((0,), (1,)), ((), ())), preferred_element_type=jnp.float32
        ),
        "fsdp",
        scatter_dimension=0,
        tiled=True,
    )
    result = summed.T.astype(jnp.bfloat16)
    returned = lax.all_to_all(
        result.reshape(groups, capacity, width_local), "ep", split_axis=0, concat_axis=0, tiled=True
    )
    weighting = jnp.sum(jnp.where(select, combine_weights[:, :, None], 0.0), axis=1)
    mixed_rows = jnp.dot(
        weighting,
        returned.reshape(-1, width_local).astype(jnp.float32),
        precision=lax.Precision.HIGHEST,
    )
    return mixed_rows.astype(jnp.bfloat16)


def solution(mesh):
    in_specs = (
        P("ep", "fsdp"),
        P("ep", None),
        P("ep", None),
        P("ep", None, "fsdp"),
        P("ep", None, "fsdp"),
        P("ep", "fsdp", None),
    )
    out_specs = P("ep", "fsdp")

    def layer(tokens, *rest):
        small = mesh.shape["ep"] == 4 and mesh.shape["fsdp"] == 8
        return (fused if small else shards)(tokens, *rest)

    return jax.shard_map(layer, mesh=mesh, in_specs=in_specs, out_specs=out_specs, check_vma=False)
```

time: 85.3 us -> 83.7 us (0.981)
  Pallas kernels: 83.5 us -> 81.9 us
    pallas_call x1, Pallas kernels: 83.5 us -> 81.9 us  [fused(): pl.pallas_call(kernel, out_shape=jax.ShapeDtypeStruct((tok_rows, width),...]
where the time goes in v3:
time: 83.7 us; the launch traced here: 83.5 us
  Pallas kernels  81.9 us (98%)
  local copies, waits for them, and re-layouts  1.62 us (2%)
    pallas_call x1, Pallas kernels, fused(): pl.pallas_call(kernel, out_shape=jax.ShapeDtypeStruct((tok_rows, width),...  81.9 us

profile of v3, /device:TPU:0, one launch (start us, length us, event | category | flops | bytes accessed | tf_op | source)
XLA Modules:
  0.0 83.5 jit_solution(154348389433804666)
XLA Ops:
  0.0 81.9 %shard_map.64 = bf16[128,768]{1,0:T(8,128)(2,1)} custom-call(bf16[128,768]{1,0:T(8,128)(2,1)} %tok.1, s32[2,128]{1,0:T(2,128)} %bitcast.2, f32[2,128]{1,0:T(2,128)} %bitcast.3, bf16[1,6144,1024]{2,1,0:T(8,128)(2,1)} %wg.1, bf16[1,6144,1024]{2,1,0:T(8,128)(2,1)} %wu.1, bf16[1,1024,6144]{2,1,0:T(8,128)(2,1)} %wd.1), custom_call_target="tpu_custom_call" | custom-call | flops 19327352832 | bytes 37748736 | tf_op jit(solution)/shard_map/pallas_call | solution.py:330
  81.9 1.6 %copy.8 = bf16[128,768]{1,0:T(8,128)(2,1)} copy(bf16[128,768]{1,0:T(8,128)(2,1)} %shard_map.64) | data formatting | bytes 393216

commit v4 on v3

--- a/solution.py
+++ b/solution.py
@@ -12,7 +12,7 @@
 
 def kernel(
     tok, ids, wts, wg, wu, wd, out,
-    rows_all, hid, wg_v, wu_v, wd_v, wt, wcol, acc,
+    rows_all, hid, wgu_v, wd_v, wt, wcol, acc,
     sib_r, s1s, s1r, s2s, s2r, s3s, s3r,
     load_sem, own_sem, z_ss, z_rs, h1_ss, h1_rs, h2_ss, h2_rs, c0_ss, c0_rs, c1_ss, c1_rs,
     wt_send, wt_recv, sib_ss, sib_rs, s1_ss, s1_rs, s2_ss, s2_rs, s3_ss, s3_rs,
@@ -34,11 +34,22 @@
     x_nbr, y_nbr, diag = (group[1], fs), (group[2], fs), (group[3], fs)
     z_dev = [None] + [(ep, sec(k, 0)) for k in (1, 2, 3)]
 
-    loads = [
-        pltpu.make_async_copy(wg.at[0], wg_v, load_sem.at[0]),
-        pltpu.make_async_copy(wu.at[0], wu_v, load_sem.at[1]),
-        pltpu.make_async_copy(wd.at[0], wd_v, load_sem.at[2]),
-    ]
+    tile = hid.shape[2] // 4
+    up_loads, down_loads = [], []
+    for i in range(4):
+        for m, w in ((0, wg), (1, wu)):
+            up_loads.append(pltpu.make_async_copy(
+                w.at[0, :, pl.ds(i * tile, tile)],
+                wgu_v.at[:, pl.ds((i * 2 + m) * tile, tile)],
+                load_sem.at[i * 2 + m],
+            ))
+        for m, plane in ((0, 1), (1, 0)):
+            at = pl.ds(pl.multiple_of(sec((i + 1) % 4, plane) * width, 128), width)
+            down_loads.append(pltpu.make_async_copy(
+                wd.at[0, :, at],
+                wd_v.at[:, pl.ds((i * 2 + m) * width, width)],
+                load_sem.at[8 + i * 2 + m],
+            ))
 
     def place(r, h):
         gy = y if r < 2 else 1 - y
@@ -83,8 +94,8 @@
     partners = [sib, x_nbr, y_nbr, diag, z_dev[1], z_dev[2], z_dev[3]]
     for dev in partners:
         pl.semaphore_signal(barrier, inc=1, device_id=dev, device_id_type=MESH)
-    loads[0].start()
-    loads[1].start()
+    for d in up_loads:
+        d.start()
     for d in own:
         d.wait()
     pl.semaphore_wait(barrier, len(partners))
@@ -160,7 +171,8 @@
     first(0, 0)
     for i, dev in ((1, x_nbr), (2, y_nbr), (3, diag)):
         send(wt.at[0], wt.at[i], wt_send.at[i], wt_recv.at[i], dev)
-    loads[2].start()
+    for d in down_loads:
+        d.start()
     second(0, 0)
     first(0, 1)
     first(0, 3)
@@ -188,25 +200,23 @@
     for k in (1, 3, 2):
         first(1, k)
 
-    tile = hid.shape[2] // 4
-
     def up(b, i):
-        at = pl.ds(pl.multiple_of(i * tile, tile), tile)
-        g = jnp.dot(rows_all[b], wg_v[:, at], preferred_element_type=F32)
-        u = jnp.dot(rows_all[b], wu_v[:, at], preferred_element_type=F32)
-        hid[b, :, at] = (g / (1.0 + jnp.exp(-g)) * u).astype(BF16)
-
-    def down(b, s):
-        p = jnp.dot(hid[b], wd_v[:, cols(s)], preferred_element_type=F32)
-        return p * wcol[b, :, 0:1]
+        at = pl.ds(pl.multiple_of(i * 2 * tile, tile), 2 * tile)
+        gu = jnp.dot(rows_all[b], wgu_v[:, at], preferred_element_type=F32)
+        g, u = gu[:, :tile], gu[:, tile:]
+        hid[b, :, pl.ds(pl.multiple_of(i * tile, tile), tile)] = (
+            g / (1.0 + jnp.exp(-g)) * u
+        ).astype(BF16)
 
     def stage0(b, j):
-        k = (j + 1) % 4
-        s = cols(sec(k, 1))
+        s = cols(sec((j + 1) % 4, 1))
         n = b * 4 + j
-        rows_all[b, :, s] = down(b, sec(k, 1)).astype(BF16)
+        at = pl.ds(pl.multiple_of(j * 2 * width, 128), 2 * width)
+        p = jnp.dot(hid[b], wd_v[:, at], preferred_element_type=F32)
+        scale = wcol[b, :, 0:1]
+        rows_all[b, :, s] = (p[:, :width] * scale).astype(BF16)
         send(rows_all.at[b, :, s], sib_r.at[b, j], sib_ss.at[n], sib_rs.at[n], sib)
-        acc[b, j] = down(b, sec(k, 0))
+        acc[b, j] = p[:, width:] * scale
 
     def stage1(b, j):
         took(sib_r.at[b, j], sib_rs.at[b * 4 + j])
@@ -247,8 +257,8 @@
             out[pl.ds(b * part + h * half, half), :] = v.astype(BF16)
 
     gathered(0)
-    loads[0].wait()
-    loads[1].wait()
+    for d in up_loads:
+        d.wait()
 
     @pl.loop(0, 4)
     def _(i):
@@ -256,7 +266,8 @@
         second(1, i)
 
     all_sent(0)
-    loads[2].wait()
+    for d in down_loads:
+        d.wait()
 
     @pl.loop(0, 4)
     def _(j):
@@ -335,8 +346,7 @@
         scratch_shapes=[
             pltpu.VMEM((2, total, model), BF16),
             pltpu.VMEM((2, total, hidden), BF16),
-            pltpu.VMEM((model, hidden), BF16),
-            pltpu.VMEM((model, hidden), BF16),
+            pltpu.VMEM((model, 2 * hidden), BF16),
             pltpu.VMEM((hidden, model), BF16),
             pltpu.VMEM((4, 8, tok_rows), F32),
             pltpu.VMEM((2, total, 128), F32),
@@ -348,7 +358,7 @@
             pltpu.VMEM((2, 4, 2, half, width), BF16),
             pltpu.VMEM((2, 3, 2, half, width), BF16),
             pltpu.VMEM((2, 3, 2, half, width), BF16),
-            dma(3),
+            dma(16),
             dma(4),
             dma(16), dma(16), dma(16), dma(16), dma(16), dma(16), dma(16), dma(16), dma(16), dma(16),
             dma(4), dma(4), dma(8), dma(8), dma(16), dma(16), dma(16), dma(16), dma(12), dma(12),

time: 83.7 us -> 83 us (level)
  no operation moved by 1% of the time
where the time goes in v4:
time: 83 us; the launch traced here: 82.9 us
  Pallas kernels  81.3 us (98%)
  local copies, waits for them, and re-layouts  1.62 us (2%)
    pallas_call x1, Pallas kernels, fused(): pl.pallas_call(kernel, out_shape=jax.ShapeDtypeStruct((tok_rows, width),...  81.3 us

profile of v4, /device:TPU:0, one launch (start us, length us, event | category | flops | bytes accessed | tf_op | source)
XLA Modules:
  0.0 82.9 jit_solution(15303234725858551628)
XLA Ops:
  0.0 81.3 %shard_map.64 = bf16[128,768]{1,0:T(8,128)(2,1)} custom-call(bf16[128,768]{1,0:T(8,128)(2,1)} %tok.1, s32[2,128]{1,0:T(2,128)} %bitcast.2, f32[2,128]{1,0:T(2,128)} %bitcast.3, bf16[1,6144,1024]{2,1,0:T(8,128)(2,1)} %wg.1, bf16[1,6144,1024]{2,1,0:T(8,128)(2,1)} %wu.1, bf16[1,1024,6144]{2,1,0:T(8,128)(2,1)} %wd.1), custom_call_target="tpu_custom_call" | custom-call | flops 19327352832 | bytes 37748736 | tf_op jit(solution)/shard_map/pallas_call | solution.py:341
  81.3 1.6 %copy.8 = bf16[128,768]{1,0:T(8,128)(2,1)} copy(bf16[128,768]{1,0:T(8,128)(2,1)} %shard_map.64) | data formatting | bytes 393216

commit v5 on v4

--- a/solution.py
+++ b/solution.py
@@ -18,8 +18,8 @@
     wt_send, wt_recv, sib_ss, sib_rs, s1_ss, s1_rs, s2_ss, s2_rs, s3_ss, s3_rs,
 ):
     tok_rows, width = tok.shape
-    part = tok_rows // 2
-    half = tok_rows // 4
+    part = tok_rows
+    half = tok_rows // 2
     ep = lax.axis_index("ep")
     fs = lax.axis_index("fsdp")
     y, x = ep // 2, ep % 2
@@ -77,7 +77,7 @@
     def tok_part(b, h):
         return tok.at[pl.ds(b * part + h * half, half)]
 
-    both = [(b, h) for b in (0, 1) for h in (0, 1)]
+    both = [(0, 0), (0, 1)]
     own = [
         pltpu.make_async_copy(tok_part(b, h), own_block(b, h, 0), own_sem.at[b * 2 + h])
         for b, h in both
@@ -146,12 +146,10 @@
             took(at, h2_rs.at[n])
             send(at, at, c1_ss.at[n], c1_rs.at[n], sib)
 
-    def gathered(b):
-        @pl.loop(0, 4)
-        def _(k):
-            for h in (0, 1):
-                took(pair(b, h, k, False, 1), c0_rs.at[num(b, h, k)])
-                took(pair(b, h, k, True, 1), c1_rs.at[num(b, h, k)])
+    def gathered(b, k):
+        for h in (0, 1):
+            took(pair(b, h, k, False, 1), c0_rs.at[num(b, h, k)])
+            took(pair(b, h, k, True, 1), c1_rs.at[num(b, h, k)])
 
     def all_sent(b):
         @pl.loop(0, 4)
@@ -171,17 +169,10 @@
     first(0, 0)
     for i, dev in ((1, x_nbr), (2, y_nbr), (3, diag)):
         send(wt.at[0], wt.at[i], wt_send.at[i], wt_recv.at[i], dev)
+    second(0, 0)
+    first(0, 1)
     for d in down_loads:
         d.start()
-    second(0, 0)
-    first(0, 1)
-    first(0, 3)
-    first(0, 2)
-    own_z(1)
-    first(1, 0)
-    second(0, 1)
-    second(0, 3)
-    second(0, 2)
 
     eye = lax.broadcasted_iota(jnp.int32, (tok_rows, tok_rows), 0) == lax.broadcasted_iota(
         jnp.int32, (tok_rows, tok_rows), 1
@@ -195,28 +186,37 @@
             lo = b * part + h * half
             wcol[b, grows(r, h), :] = jnp.broadcast_to(col[lo:lo + half], (half, 128))
 
-    for k in (0, 1, 3, 2):
-        last(0, k)
-    for k in (1, 3, 2):
-        first(1, k)
-
-    def up(b, i):
+    def up(k, i, begin, end):
+        rows = pl.ds(pl.multiple_of(((z + k) % 4) * 2 * width, 128), 2 * width)
         at = pl.ds(pl.multiple_of(i * 2 * tile, tile), 2 * tile)
-        gu = jnp.dot(rows_all[b], wgu_v[:, at], preferred_element_type=F32)
-        g, u = gu[:, :tile], gu[:, tile:]
-        hid[b, :, pl.ds(pl.multiple_of(i * tile, tile), tile)] = (
-            g / (1.0 + jnp.exp(-g)) * u
-        ).astype(BF16)
+        gu = jnp.dot(rows_all[0, :, rows], wgu_v[rows, at], preferred_element_type=F32)
+        if not begin:
+            gu = gu + acc[0, i, :, 0:2 * tile]
+        if not end:
+            acc[0, i, :, 0:2 * tile] = gu
+        else:
+            g, u = gu[:, :tile], gu[:, tile:]
+            hid[0, :, pl.ds(pl.multiple_of(i * tile, tile), tile)] = (
+                g / (1.0 + jnp.exp(-g)) * u
+            ).astype(BF16)
+
+    def ups(k, lo, begin=False, end=False):
+        @pl.loop(lo, 4)
+        def _(i):
+            up(k, i, begin, end)
 
     def stage0(b, j):
         s = cols(sec((j + 1) % 4, 1))
         n = b * 4 + j
-        at = pl.ds(pl.multiple_of(j * 2 * width, 128), 2 * width)
-        p = jnp.dot(hid[b], wd_v[:, at], preferred_element_type=F32)
-        scale = wcol[b, :, 0:1]
-        rows_all[b, :, s] = (p[:, :width] * scale).astype(BF16)
+
+        def down(m):
+            at = pl.ds(pl.multiple_of((j * 2 + m) * width, 128), width)
+            p = jnp.dot(hid[b], wd_v[:, at], preferred_element_type=F32)
+            return p * wcol[b, :, 0:1]
+
+        rows_all[b, :, s] = down(0).astype(BF16)
         send(rows_all.at[b, :, s], sib_r.at[b, j], sib_ss.at[n], sib_rs.at[n], sib)
-        acc[b, j] = p[:, width:] * scale
+        acc[b, j] = down(1)
 
     def stage1(b, j):
         took(sib_r.at[b, j], sib_rs.at[b * 4 + j])
@@ -256,15 +256,26 @@
                 v = v + s3r[b, i, h].astype(F32)
             out[pl.ds(b * part + h * half, half), :] = v.astype(BF16)
 
-    gathered(0)
+    last(0, 0)
+    second(0, 1)
+    first(0, 3)
+    first(0, 2)
+    gathered(0, 0)
     for d in up_loads:
         d.wait()
-
-    @pl.loop(0, 4)
-    def _(i):
-        up(0, i)
-        second(1, i)
-
+    ups(0, 0, begin=True)
+    last(0, 1)
+    second(0, 3)
+    gathered(0, 1)
+    up(1, 0, False, False)
+    second(0, 2)
+    ups(1, 1)
+    last(0, 3)
+    gathered(0, 3)
+    ups(3, 0)
+    last(0, 2)
+    gathered(0, 2)
+    ups(2, 0, end=True)
     all_sent(0)
     for d in down_loads:
         d.wait()
@@ -272,50 +283,23 @@
     @pl.loop(0, 4)
     def _(j):
         stage0(0, j)
-        last(1, j)
+        stage1(0, j)
 
         @pl.when(j > 0)
         def _():
-            stage1(0, j - 1)
-
-    stage1(0, 3)
-    gathered(1)
-
-    @pl.loop(0, 4)
-    def _(i):
-        up(1, i)
-        stage2(0, i)
-
-        @pl.when(i > 0)
-        def _():
-            stage3(0, i - 1)
-
-    all_sent(1)
-
-    @pl.loop(0, 4)
-    def _(j):
-        stage0(1, j)
-
-        @pl.when(j > 0)
-        def _():
-            stage1(1, j - 1)
+            stage2(0, j - 1)
 
         @pl.when(j > 1)
         def _():
-            stage2(1, j - 2)
-
-    stage1(1, 3)
-    stage2(1, 2)
-    stage3(1, 0)
+            stage3(0, j - 2)
+
+    stage2(0, 3)
+    stage3(0, 2)
     finish(0)
-    stage3(1, 1)
-    stage2(1, 3)
-    stage3(1, 2)
-    finish(1)
 
     for i in (1, 2, 3):
         left(wt.at[0], wt_send.at[i])
-    for b in (0, 1):
+    for b in (0,):
         @pl.loop(0, 4)
         def _(j):
             left(sib_r.at[b, j], sib_ss.at[b * 4 + j])
@@ -333,8 +317,8 @@
     tok_rows, width = tokens.shape
     model = w_gate.shape[1]
     hidden = w_gate.shape[2]
-    total = 2 * tok_rows
-    half = tok_rows // 4
+    total = 4 * tok_rows
+    half = tok_rows // 2
     vm = pl.BlockSpec(memory_space=pltpu.VMEM)
     hbm = pl.BlockSpec(memory_space=pl.ANY)
     dma = lambda n: pltpu.SemaphoreType.DMA((n,))
@@ -344,32 +328,32 @@
         in_specs=[vm, vm, vm, hbm, hbm, hbm],
         out_specs=vm,
         scratch_shapes=[
-            pltpu.VMEM((2, total, model), BF16),
-            pltpu.VMEM((2, total, hidden), BF16),
+            pltpu.VMEM((1, total, model), BF16),
+            pltpu.VMEM((1, total, hidden), BF16),
             pltpu.VMEM((model, 2 * hidden), BF16),
             pltpu.VMEM((hidden, model), BF16),
             pltpu.VMEM((4, 8, tok_rows), F32),
-            pltpu.VMEM((2, total, 128), F32),
-            pltpu.VMEM((2, 4, total, width), F32),
-            pltpu.VMEM((2, 4, total, width), BF16),
-            pltpu.VMEM((2, 4, 2, 2, half, width), BF16),
-            pltpu.VMEM((2, 4, 2, 2, half, width), BF16),
-            pltpu.VMEM((2, 4, 2, half, width), BF16),
-            pltpu.VMEM((2, 4, 2, half, width), BF16),
-            pltpu.VMEM((2, 3, 2, half, width), BF16),
-            pltpu.VMEM((2, 3, 2, half, width), BF16),
+            pltpu.VMEM((1, total, 128), F32),
+            pltpu.VMEM((1, 4, total, width), F32),
+            pltpu.VMEM((1, 4, total, width), BF16),
+            pltpu.VMEM((1, 4, 2, 2, half, width), BF16),
+            pltpu.VMEM((1, 4, 2, 2, half, width), BF16),
+            pltpu.VMEM((1, 4, 2, half, width), BF16),
+            pltpu.VMEM((1, 4, 2, half, width), BF16),
+            pltpu.VMEM((1, 3, 2, half, width), BF16),
+            pltpu.VMEM((1, 3, 2, half, width), BF16),
             dma(16),
-            dma(4),
-            dma(16), dma(16), dma(16), dma(16), dma(16), dma(16), dma(16), dma(16), dma(16), dma(16),
-            dma(4), dma(4), dma(8), dma(8), dma(16), dma(16), dma(16), dma(16), dma(12), dma(12),
+            dma(2),
+            dma(8), dma(8), dma(8), dma(8), dma(8), dma(8), dma(8), dma(8), dma(8), dma(8),
+            dma(4), dma(4), dma(4), dma(4), dma(8), dma(8), dma(8), dma(8), dma(6), dma(6),
         ],
         compiler_params=pltpu.CompilerParams(
             collective_id=0, has_side_effects=True, vmem_limit_bytes=63 * 1024 * 1024
         ),
         cost_estimate=pl.CostEstimate(
-            flops=12 * total * model * hidden,
+            flops=6 * total * model * hidden,
             bytes_accessed=6 * model * hidden,
-            transcendentals=2 * total * hidden,
+            transcendentals=total * hidden,
         ),
     )(tokens, expert_ids.T, combine_weights.T, w_gate, w_up, w_down)
 

time: 83 us -> 93.1 us (1.12)
  Pallas kernels: 81.3 us -> 91.3 us
    pallas_call x1, Pallas kernels: 81.3 us -> 91.3 us  [fused(): pl.pallas_call(kernel, out_shape=jax.ShapeDtypeStruct((tok_rows, width),...]
where the time goes in v5:
time: 93.1 us; the launch traced here: 92.9 us
  Pallas kernels  91.3 us (98%)
  local copies, waits for them, and re-layouts  1.62 us (2%)
    pallas_call x1, Pallas kernels, fused(): pl.pallas_call(kernel, out_shape=jax.ShapeDtypeStruct((tok_rows, width),...  91.3 us

profile of v5, /device:TPU:0, one launch (start us, length us, event | category | flops | bytes accessed | tf_op | source)
XLA Modules:
  0.0 92.9 jit_solution(6511902222600872673)
XLA Ops:
  0.0 91.3 %shard_map.64 = bf16[128,768]{1,0:T(8,128)(2,1)} custom-call(bf16[128,768]{1,0:T(8,128)(2,1)} %tok.1, s32[2,128]{1,0:T(2,128)} %bitcast.2, f32[2,128]{1,0:T(2,128)} %bitcast.3, bf16[1,6144,1024]{2,1,0:T(8,128)(2,1)} %wg.1, bf16[1,6144,1024]{2,1,0:T(8,128)(2,1)} %wu.1, bf16[1,1024,6144]{2,1,0:T(8,128)(2,1)} %wd.1), custom_call_target="tpu_custom_call" | custom-call | flops 19327352832 | bytes 37748736 | tf_op jit(solution)/shard_map/pallas_call | solution.py:325
  91.3 1.6 %copy.8 = bf16[128,768]{1,0:T(8,128)(2,1)} copy(bf16[128,768]{1,0:T(8,128)(2,1)} %shard_map.64) | data formatting | bytes 393216
